TPU v7x, 512 devices: a whole 4x8x8 slice. The times are simulated.
512 devices in a mesh: dom: 64 (over y, x, core), feat: 8 (over z).
Axes of the slice: x: 4, y: 8, z: 8, core: 2. Of those that a mesh axis runs over, the one named last changes fastest.
Arguments:
- features: bfloat16 [512, 196608], P('feat', 'dom'), may hold values from -16 to 16
- weights: bfloat16 [2, 512, 512], replicated, may hold values from -0.1875 to 0.1875
- tile_values: bfloat16 [4608, 128, 128], P('dom'), may hold values from 0 to 0.099609375
- tile_blocks: int32 [4608, 2], P('dom'), may hold values from 0 to 31
- tile_counts: int32 [64], P('dom'), may hold values from 36 to 72
- replica: int32 [64, 64, 16], P('dom'), may hold values from -1 to 3071, as said below
- cotangent: bfloat16 [512, 196608], P(None, ('dom', 'feat')), may hold values from -6 to 6
Outputs:
- output: bfloat16 [512, 196608], P(None, ('dom', 'feat'))
- feature_grad: bfloat16 [512, 196608], P('feat', 'dom')
- weight_grad: float32 [2, 512, 512], P(None, 'feat')
Inputs may be any that keep to these rules, and one draw needn't show every extreme that they name: `tile_blocks`: column 0 names a tile's source block and column 1 its destination block. replica[q, p, k] is the master slot on partition q of the vertex in mirror slot q * 16 + k of partition p, or -1 for an unused slot; the used slots of a pair (q, p) come first; no partition mirrors its own masters; each master partition fills all 16 slots toward at least one partition.
All inputs are finite; a program needn't handle non-finite values.
Results may differ from a plain program's by a relative error of at most 0.0058.
Values may be sent and summed in bfloat16 or wider, within the bound.
A program may use at most 64 MiB of HBM per device.

v0:
```python
import jax
import jax.numpy as jnp
from jax import lax
from jax.sharding import PartitionSpec as P


def gathered_total(x, axis):
    pieces = lax.all_gather(x, axis).astype(jnp.float32)
    return pieces.sum(axis=0)


def local(features, weights, tile_values, tile_blocks, tile_counts, replica, cotangent):
    feat_width, masters = features.shape
    tile_size = tile_values.shape[1]
    replica_rows = replica[0]
    slot_used = (replica_rows >= 0).reshape(-1)
    slot_index = jnp.where(replica_rows >= 0, replica_rows, 0).reshape(-1)
    tile_live = (jnp.arange(tile_values.shape[0]) < tile_counts[0]).astype(jnp.float32)
    source_blocks = tile_blocks[:, 0]
    target_blocks = tile_blocks[:, 1]

    def pull_mirrors(values_in):
        outgoing = jnp.where(
            slot_used[None, :],
            jnp.take(values_in, slot_index, axis=1),
            jnp.zeros((), values_in.dtype),
        )
        return lax.all_to_all(outgoing, "dom", split_axis=1, concat_axis=1, tiled=True)

    def push_mirrors(partial_value):
        incoming = lax.all_to_all(
            partial_value[:, masters:].astype(jnp.bfloat16),
            "dom",
            split_axis=1,
            concat_axis=1,
            tiled=True,
        ).astype(jnp.float32)
        targets = jnp.where(slot_used, slot_index, masters)
        return partial_value[:, :masters].at[:, targets].add(incoming, mode="drop")

    def spread(own_cols, forward):
        local_cols = jnp.concatenate([own_cols, pull_mirrors(own_cols)], 1)
        nblocks = local_cols.shape[1] // tile_size
        blocks = local_cols.reshape(feat_width, nblocks, tile_size)
        if forward:
            picked = jnp.take(blocks, source_blocks, axis=1)
            contrib = jnp.einsum(
                "fts,tsd->ftd", picked, tile_values, preferred_element_type=jnp.float32
            )
            segment = target_blocks
        else:
            picked = jnp.take(blocks, target_blocks, axis=1)
            contrib = jnp.einsum(
                "ftd,tsd->fts", picked, tile_values, preferred_element_type=jnp.float32
            )
            segment = source_blocks
        onehot = (segment[:, None] == jnp.arange(nblocks)[None, :]).astype(jnp.float32) * tile_live[
            :, None
        ]
        partial_value = jnp.einsum("ftd,tb->fbd", contrib, onehot, precision=lax.Precision.HIGHEST)
        return push_mirrors(partial_value.reshape(feat_width, nblocks * tile_size))

    aggregate = spread(features, True).astype(jnp.bfloat16)
    feat_rows, agg_rows = (
        lax.all_to_all(features, "feat", split_axis=1, concat_axis=0, tiled=True),
        lax.all_to_all(aggregate, "feat", split_axis=1, concat_axis=0, tiled=True),
    )
    preact = jnp.einsum("io,iv->ov", weights[0], feat_rows, preferred_element_type=jnp.float32)
    preact = preact + jnp.einsum(
        "io,iv->ov", weights[1], agg_rows, preferred_element_type=jnp.float32
    )
    sigmoid_z = jax.nn.sigmoid(preact)
    output = (preact * sigmoid_z).astype(jnp.bfloat16)
    slope = sigmoid_z * (1.0 + preact * (1.0 - sigmoid_z))
    pre_grad = (cotangent.astype(jnp.float32) * slope).astype(jnp.bfloat16)
    slice_start = lax.axis_index("feat") * feat_width
    grad_cols = lax.all_gather(pre_grad, "feat", axis=1, tiled=True)
    weight_slice = lax.dynamic_slice_in_dim(weights, slice_start, feat_width, 1)
    terms = jnp.stack(
        [
            jnp.einsum("iv,ov->io", features, grad_cols, preferred_element_type=jnp.float32),
            jnp.einsum("iv,ov->io", aggregate, grad_cols, preferred_element_type=jnp.float32),
        ]
    )
    weight_grad = gathered_total(terms.astype(jnp.bfloat16), "dom").astype(jnp.float32)
    back_slices = jnp.einsum(
        "kio,ov->kiv", weight_slice, grad_cols, preferred_element_type=jnp.float32
    ).astype(jnp.bfloat16)
    self_grad = back_slices[0]
    agg_grad = back_slices[1]
    back_terms = spread(agg_grad, False)
    feature_grad = (self_grad.astype(jnp.float32) + back_terms).astype(jnp.bfloat16)
    return (output, feature_grad, weight_grad)


def solution(mesh):
    return jax.shard_map(
        local,
        mesh=mesh,
        in_specs=(
            P("feat", "dom"),
            P(),
            P("dom", None, None),
            P("dom", None),
            P("dom"),
            P("dom", None, None),
            P(None, ("dom", "feat")),
        ),
        out_specs=(P(None, ("dom", "feat")), P("feat", "dom"), P(None, "feat", None)),
        check_vma=False,
    )
```

profile of v0, /device:TPU:1, one launch (start us, length us, event | category | flops | bytes accessed | tf_op | source)
XLA Modules:
  0.0 258.0 jit_solution(7112404868492813658)
XLA Ops:
  7.2 0.9 copy.71
  8.8 1.4 copy.72
  10.1 4.3 %gather_fusion = bf16[1024,64]{1,0:T(8,128)(2,1)} fusion(bf16[64,3072]{0,1:T(8,128)(2,1)S(1)} %copy.72, s32[1024]{0:T(1024)S(1)} %fusion.34), kind=kCustom, calls=%fused_computation.clone | custom fusion | bytes 266240 | tf_op jit(solution)/shard_map/jit(_take)/gather | solution.py:25
  14.5 1.3 bitcast_select_fusion.1
  15.8 0.8 reshape.201
  16.6 11.6 %all-to-all-start.1 = ((bf16[64,2,512]{2,1,0:T(2,128)(2,1)}), bf16[64,2,512]{2,1,0:T(2,128)(2,1)S(1)}, u32[]{:S(2)}, u32[]{:S(2)}) async-start(bf16[64,2,512]{2,1,0:T(2,128)(2,1)} %reshape.201), calls=%async_computation.1 | async-start | bytes 262144 | tf_op jit(solution)/shard_map/all_to_all | solution.py:28
  29.5 1.3 slice_bitcast_fusion.2
  30.8 8.6 %all-to-all-done.1 = bf16[64,2,512]{2,1,0:T(2,128)(2,1)S(1)} async-done(((bf16[64,2,512]{2,1,0:T(2,128)(2,1)}), bf16[64,2,512]{2,1,0:T(2,128)(2,1)S(1)}, u32[]{:S(2)}, u32[]{:S(2)}) %all-to-all-start.1) | async-done | bytes 131104 | tf_op jit(solution)/shard_map/all_to_all | solution.py:28
  39.9 1.8 gather_fusion.1
  41.7 2.1 convolution_bitcast_fusion.1
  43.8 2.7 %fusion.3 = f32[32,64,128]{2,0,1:T(8,128)S(1)} fusion(f32[64,72,128]{2,0,1:T(8,128)S(1)} %convolution_bitcast_fusion.1, f32[72]{0:T(128)S(1)} %compare_convert_fusion, s32[72]{0:T(128)S(1)} %get-tuple-element.29), kind=kOutput, calls=%fused_computation.11 | convolution fusion | flops 226497024 | bytes 3408448 | tf_op jit(solution)/shard_map/ftd,tb->fbd/dot_general | solution.py:60
  47.1 1.0 copy-done.3
  48.3 0.8 reshape.203
  49.1 4.4 %all-to-all-start.2 = ((bf16[64,2,512]{2,1,0:T(2,128)(2,1)}), bf16[64,2,512]{2,1,0:T(2,128)(2,1)S(1)}, u32[]{:S(2)}, u32[]{:S(2)}) async-start(bf16[64,2,512]{2,1,0:T(2,128)(2,1)} %reshape.203), calls=%async_computation.2 | async-start | bytes 262144 | tf_op jit(solution)/shard_map/all_to_all | solution.py:31
  54.3 10.6 %all-to-all-done.2 = bf16[64,2,512]{2,1,0:T(2,128)(2,1)S(1)} async-done(((bf16[64,2,512]{2,1,0:T(2,128)(2,1)}), bf16[64,2,512]{2,1,0:T(2,128)(2,1)S(1)}, u32[]{:S(2)}, u32[]{:S(2)}) %all-to-all-start.2) | async-done | bytes 131104 | tf_op jit(solution)/shard_map/all_to_all | solution.py:31
  64.9 10.0 %all-to-all-start = ((bf16[64,8,384]{2,0,1:T(8,128)(2,1)}), bf16[64,8,384]{2,0,1:T(8,128)(2,1)}, u32[]{:S(2)}, u32[]{:S(2)}) async-start(bf16[64,8,384]{2,0,1:T(8,128)(2,1)} %bitcast.122), calls=%async_computation | async-start | bytes 786432 | tf_op jit(solution)/shard_map/all_to_all | solution.py:65
  75.6 1.2 slice.50
  76.8 1.6 copy.78
  78.5 1.1 reshape.204
  79.6 8.2 %scatter_custom_fusion = f32[64,3072]{0,1:T(8,128)} fusion(f32[64,3072]{0,1:T(8,128)} %copy.78, s32[1024]{0:T(1024)} %bitcast.140, bf16[64,1024]{0,1:T(8,128)(2,1)S(1)} %bitcast.133), kind=kCustom, calls=%fused_computation.42 | custom fusion | flops 131072 | bytes 917504 | tf_op jit(solution)/shard_map/scatter-add | solution.py:39
  87.8 1.5 convert_element_type.61
  89.3 1.0 copy.79
  90.3 6.6 %all-to-all-start.3 = ((bf16[64,8,384]{2,0,1:T(8,128)(2,1)}), bf16[64,8,384]{2,0,1:T(8,128)(2,1)}, u32[]{:S(2)}, u32[]{:S(2)}) async-start(bf16[64,8,384]{2,0,1:T(8,128)(2,1)} %copy.79), calls=%async_computation.3 | async-start | bytes 786432 | tf_op jit(solution)/shard_map/all_to_all | solution.py:66
  97.2 2.5 fusion.19
  99.7 10.8 %all-to-all-done.3 = bf16[64,8,384]{2,0,1:T(8,128)(2,1)} async-done(((bf16[64,8,384]{2,0,1:T(8,128)(2,1)}), bf16[64,8,384]{2,0,1:T(8,128)(2,1)}, u32[]{:S(2)}, u32[]{:S(2)}) %all-to-all-start.3) | async-done | bytes 393248 | tf_op jit(solution)/shard_map/all_to_all | solution.py:66
  110.4 3.1 %multiply_convert_fusion = (bf16[512,384]{1,0:T(8,128)(2,1)}, bf16[512,384]{1,0:T(8,128)(2,1)}) fusion(bf16[512,384]{1,0:T(8,128)(2,1)} %param.17, f32[512,384]{1,0:T(8,128)} %fusion.19, bf16[512,384]{1,0:T(8,128)(2,1)} %bitcast.19, bf16[2,512,512]{2,1,0:T(8,128)(2,1)} %param.12), kind=kOutput, calls=%fused_computation.30 | convolution fusion | flops 203882496 | bytes 2883584 | tf_op jit(solution)/shard_map/io,iv->ov/dot_general | solution.py:69
  113.6 38.6 %all-gather.3.cloned.1.call-done = bf16[512,3072]{1,0:T(8,128)(2,1)} async-done(((bf16[512,384]{1,0:T(8,128)(2,1)}), bf16[512,3072]{1,0:T(8,128)(2,1)}) %all-gather.3.cloned.1.call-update) | async-done | bytes 3145744 | tf_op jit(solution)/shard_map/all_gather | solution.py:77
  152.2 3.1 %fusion.13 = bf16[1,1,64,512]{3,2,1,0:T(8,128)(2,1)S(1)} fusion(bf16[64,3072]{0,1:T(8,128)(2,1)S(1)} %convert_element_type.61, bf16[512,3072]{1,0:T(8,128)(2,1)} %all-gather.3.cloned.1.call-done), kind=kOutput, calls=%fused_computation.26 | convolution fusion | flops 201359360 | bytes 3604480 | tf_op jit(solution)/shard_map/iv,ov->io/dot_general | solution.py:82
  155.3 1.1 fusion.12
  157.1 2.6 convolution_convert_fusion
  159.7 0.9 copy-done.4
  161.0 4.3 %gather_fusion.2 = bf16[1024,64]{1,0:T(8,128)(2,1)} fusion(bf16[64,3072]{0,1:T(8,128)(2,1)S(1)} %copy.81, s32[1024]{0:T(1024)S(1)} %fusion.34), kind=kCustom, calls=%fused_computation.2.clone | custom fusion | bytes 266240 | tf_op jit(solution)/shard_map/jit(_take)/gather | solution.py:25
  165.3 1.3 bitcast_select_fusion
  166.8 22.9 %all_to_all.80 = bf16[64,2,512]{2,1,0:T(2,128)(2,1)S(1)} all-to-all(bf16[64,2,512]{2,1,0:T(2,128)(2,1)S(1)} %reshape.205), channel_id=1, replica_groups=mesh['dom'=64,'feat'=8] {'dom'}, dimensions={0} | all-to-all | bytes 262144 | tf_op jit(solution)/shard_map/all_to_all | solution.py:28
  190.2 1.9 gather_fusion.3
  192.1 3.0 %convolution_bitcast_fusion = f32[64,72,128]{2,0,1:T(8,128)S(1)} fusion(bf16[72,128,128]{2,1,0:T(8,128)(2,1)S(1)} %copy-done, bf16[72,64,128]{2,1,0:T(8,128)(2,1)} %gather_fusion.3, pred[72]{0:T(512)(128)(4,1)S(1)} %copy-done.11), kind=kOutput, calls=%fused_computation.13 | convolution fusion | flops 151584768 | bytes 5898312 | tf_op jit(solution)/shard_map/ftd,tsd->fts/dot_general | solution.py:53
  195.1 2.7 %fusion.1 = f32[32,64,128]{2,0,1:T(8,128)S(1)} fusion(f32[64,72,128]{2,0,1:T(8,128)S(1)} %convolution_bitcast_fusion, s32[72]{0:T(128)S(1)} %copy-done.12, f32[72]{0:T(128)S(1)} %copy-done.10), kind=kOutput, calls=%fused_computation.9 | convolution fusion | flops 226497024 | bytes 3408448 | tf_op jit(solution)/shard_map/ftd,tb->fbd/dot_general | solution.py:60
  198.4 0.8 copy.85
  199.3 1.8 reshape.207
  201.0 4.5 %all-to-all-start.5 = ((bf16[64,2,512]{2,1,0:T(2,128)(2,1)}), bf16[64,2,512]{2,1,0:T(2,128)(2,1)S(1)}, u32[]{:S(2)}, u32[]{:S(2)}) async-start(bf16[64,2,512]{2,1,0:T(2,128)(2,1)} %reshape.207), calls=%async_computation.5 | async-start | bytes 262144 | tf_op jit(solution)/shard_map/all_to_all | solution.py:31
  205.5 1.9 slice_add_fusion
  207.5 2.8 %copy.86 = f32[64,3072]{0,1:T(8,128)} copy(f32[64,3072]{1,0:T(8,128)} %slice_add_fusion) | data formatting | bytes 1572864 | tf_op jit(solution)/shard_map/add
  210.3 6.6 %all-to-all-done.5 = bf16[64,2,512]{2,1,0:T(2,128)(2,1)S(1)} async-done(((bf16[64,2,512]{2,1,0:T(2,128)(2,1)}), bf16[64,2,512]{2,1,0:T(2,128)(2,1)S(1)}, u32[]{:S(2)}, u32[]{:S(2)}) %all-to-all-start.5) | async-done | bytes 131104 | tf_op jit(solution)/shard_map/all_to_all | solution.py:31
  217.1 8.2 %scatter_custom_fusion.1 = f32[64,3072]{0,1:T(8,128)} fusion(f32[64,3072]{0,1:T(8,128)} %copy.86, s32[1024]{0:T(1024)} %bitcast.141, bf16[64,1024]{0,1:T(8,128)(2,1)S(1)} %bitcast.132), kind=kCustom, calls=%fused_computation.40 | custom fusion | flops 131072 | bytes 917504 | tf_op jit(solution)/shard_map/scatter-add | solution.py:39
  225.3 1.5 convert_element_type.70
  226.8 1.0 copy.87
  227.8 17.9 %all-gather.5.cloned.1.call-done = bf16[64,2,64,512]{3,2,1,0:T(8,128)(2,1)} async-done(((bf16[1,2,64,512]{3,2,1,0:T(8,128)(2,1)}), bf16[64,2,64,512]{3,2,1,0:T(8,128)(2,1)}) %all-gather.5.cloned.1.call-update) | async-done | bytes 8388624 | tf_op jit(solution)/shard_map/all_gather | solution.py:8
  245.7 5.5 %convert_reduce_fusion = f32[2,64,512]{2,1,0:T(8,128)} fusion(bf16[64,2,64,512]{3,2,1,0:T(8,128)(2,1)} %all-gather.5.cloned.1.call-done), kind=kLoop, calls=%fused_computation.6 | loop fusion | flops 8323072 | bytes 8650752 | tf_op jit(solution)/shard_map/reduce_sum | solution.py:9
  (54 shorter events, 6.8 us)
Async XLA Ops:
  7.2 34.5 %copy-start = (bf16[72,128,128]{2,1,0:T(8,128)(2,1)S(1)}, bf16[72,128,128]{2,1,0:T(8,128)(2,1)}, u32[]{:S(2)}) copy-start(bf16[72,128,128]{2,1,0:T(8,128)(2,1)} %param.13) | copy-start | bytes 7077892
  7.2 32.5 %copy-start.2 = (bf16[64,3072]{1,0:T(8,128)(2,1)S(1)}, bf16[64,3072]{1,0:T(8,128)(2,1)}, u32[]{:S(2)}) copy-start(bf16[64,3072]{1,0:T(8,128)(2,1)} %param.11) | copy-start | bytes 1179652
  7.2 21.0 %copy-start.8 = (s32[72,2]{0,1:T(2,128)S(1)}, s32[72,2]{0,1:T(2,128)}, u32[]{:S(2)}) copy-start(s32[72,2]{0,1:T(2,128)} %param.14) | copy-start | bytes 1732
  8.1 0.6 copy-start.6
  16.6 22.7 %all-to-all-start.1 = ((bf16[64,2,512]{2,1,0:T(2,128)(2,1)}), bf16[64,2,512]{2,1,0:T(2,128)(2,1)S(1)}, u32[]{:S(2)}, u32[]{:S(2)}) async-start(bf16[64,2,512]{2,1,0:T(2,128)(2,1)} %reshape.201), calls=%async_computation.1 | async-start | bytes 262144 | tf_op jit(solution)/shard_map/all_to_all | solution.py:28
  29.5 14.3 %copy-start.9 = (f32[72]{0:T(128)}, f32[72]{0:T(128)S(1)}, u32[]{:S(2)}) copy-start(f32[72]{0:T(128)S(1)} %compare_convert_fusion) | copy-start | bytes 868
  46.4 28.5 %copy-start.7 = (s32[1,64,16]{2,1,0:T(8,128)S(1)}, s32[1,64,16]{2,1,0:T(8,128)}, u32[]{:S(2)}) copy-start(s32[1,64,16]{2,1,0:T(8,128)} %copy-done.6) | copy-start | bytes 12292
  47.1 1.0 copy-start.3
  49.1 15.8 %all-to-all-start.2 = ((bf16[64,2,512]{2,1,0:T(2,128)(2,1)}), bf16[64,2,512]{2,1,0:T(2,128)(2,1)S(1)}, u32[]{:S(2)}, u32[]{:S(2)}) async-start(bf16[64,2,512]{2,1,0:T(2,128)(2,1)} %reshape.203), calls=%async_computation.2 | async-start | bytes 262144 | tf_op jit(solution)/shard_map/all_to_all | solution.py:31
  64.9 10.1 %copy-start.5 = (bf16[64,2,512]{2,1,0:T(2,128)(2,1)}, bf16[64,2,512]{2,1,0:T(2,128)(2,1)S(1)}, u32[]{:S(2)}) copy-start(bf16[64,2,512]{2,1,0:T(2,128)(2,1)S(1)} %all-to-all-done.2) | copy-start | bytes 393220
  64.9 25.4 %all-to-all-start = ((bf16[64,8,384]{2,0,1:T(8,128)(2,1)}), bf16[64,8,384]{2,0,1:T(8,128)(2,1)}, u32[]{:S(2)}, u32[]{:S(2)}) async-start(bf16[64,8,384]{2,0,1:T(8,128)(2,1)} %bitcast.122), calls=%async_computation | async-start | bytes 786432 | tf_op jit(solution)/shard_map/all_to_all | solution.py:65
  90.3 20.1 %all-to-all-start.3 = ((bf16[64,8,384]{2,0,1:T(8,128)(2,1)}), bf16[64,8,384]{2,0,1:T(8,128)(2,1)}, u32[]{:S(2)}, u32[]{:S(2)}) async-start(bf16[64,8,384]{2,0,1:T(8,128)(2,1)} %copy.79), calls=%async_computation.3 | async-start | bytes 786432 | tf_op jit(solution)/shard_map/all_to_all | solution.py:66
  96.9 55.3 %all-gather.3.cloned.1.call-start = ((), (), s32[]{:S(2)}) async-start(), calls=%async_computation.6 | async-start | bytes 3538944 | tf_op jit(solution)/shard_map/all_gather | solution.py:77
  113.6 132.1 %all-gather.5.cloned.1.call-start = ((), (), s32[]{:S(2)}) async-start(), calls=%async_computation.7 | async-start | bytes 8519680 | tf_op jit(solution)/shard_map/all_gather | solution.py:8
  152.2 3.1 %copy-start.1 = (bf16[512,3072]{1,0:T(8,128)(2,1)S(1)}, bf16[512,3072]{1,0:T(8,128)(2,1)}, u32[]{:S(2)}) copy-start(bf16[512,3072]{1,0:T(8,128)(2,1)} %all-gather.3.cloned.1.call-done) | copy-start | bytes 9437188
  159.6 0.9 copy-start.4
  166.6 25.5 %copy-start.11 = (pred[72]{0:T(512)(128)(4,1)S(1)}, pred[72]{0:T(512)(128)(4,1)}, u32[]{:S(2)}) copy-start(pred[72]{0:T(512)(128)(4,1)} %get-tuple-element.20) | copy-start | bytes 220
  192.1 3.0 %copy-start.10 = (f32[72]{0:T(128)S(1)}, f32[72]{0:T(128)}, u32[]{:S(2)}) copy-start(f32[72]{0:T(128)} %copy-done.9) | copy-start | bytes 868
  192.1 3.0 %copy-start.12 = (s32[72]{0:T(128)S(1)}, s32[72]{0:T(128)}, u32[]{:S(2)}) copy-start(s32[72]{0:T(128)} %get-tuple-element.28) | copy-start | bytes 868
  201.0 15.8 %all-to-all-start.5 = ((bf16[64,2,512]{2,1,0:T(2,128)(2,1)}), bf16[64,2,512]{2,1,0:T(2,128)(2,1)S(1)}, u32[]{:S(2)}, u32[]{:S(2)}) async-start(bf16[64,2,512]{2,1,0:T(2,128)(2,1)} %reshape.207), calls=%async_computation.5 | async-start | bytes 262144 | tf_op jit(solution)/shard_map/all_to_all | solution.py:31
Sparse Core Ops, SparseCore 0:
  113.7 38.4 all-gather.2
  157.2 88.4 all-gather.4
where the time goes:
time: 259 us; the launch traced here: 258 us
  waiting for transfers between devices  92.9 us (36%)
  starting transfers between devices  37.5 us (14%)
  local copies, waits for them, and re-layouts  35.4 us (14%)
  other arithmetic  31.5 us (12%)
  blocking collectives  22.9 us (9%)
  matrix products  22.7 us (9%)
  between operations  15 us (6%)
    all_gather x1, waiting for transfers between devices, local(): grad_cols = lax.all_gather(pre_grad, 'feat', axis=1, tiled=True)  38.6 us
    all_to_all x1, blocking collectives, pull_mirrors(): lax.all_to_all(outgoing, 'dom', split_axis=1, concat_axis=1, tiled=True)  22.9 us
    all_gather x1, waiting for transfers between devices, gathered_total(): pieces = lax.all_gather(x, axis).astype(jnp.float32)  17.9 us
    all_to_all x2, waiting for transfers between devices, push_mirrors(): lax.all_to_all(partial_value[:, masters:].astype(jnp.bfloat16), 'dom', sp...  17.1 us
    scatter-add x2, other arithmetic, push_mirrors(): return partial_value[:, :masters].at[:, targets].add(incoming, mode='drop')  16.4 us
    unnamed x39, local copies, waits for them, and re-layouts  12.5 us
    all_to_all x1, starting transfers between devices, pull_mirrors(): lax.all_to_all(outgoing, 'dom', split_axis=1, concat_axis=1, tiled=True)  11.6 us
    all_to_all x1, waiting for transfers between devices, local(): lax.all_to_all(aggregate, 'feat', split_axis=1, concat_axis=0, tiled=True)  10.8 us
  transfers between devices with their start and end apart: 7, of which 6 were waited for; matrix products, arithmetic and copies ran while one was open for 22% of the time, Pallas kernels for 0%

commit v1 on v0

--- a/solution.py
+++ b/solution.py
@@ -2,6 +2,12 @@
 import jax.numpy as jnp
 from jax import lax
 from jax.sharding import PartitionSpec as P
+
+
+def trade_parts(x, mesh_axis, split, join):
+    pieces = jnp.split(x, lax.axis_size(mesh_axis), axis=split)
+    received = lax.all_to_all(jnp.stack(pieces), mesh_axis, 0, 0)
+    return jnp.concatenate(received, axis=join)
 
 
 def gathered_total(x, axis):
@@ -62,7 +68,7 @@
 
     aggregate = spread(features, True).astype(jnp.bfloat16)
     feat_rows, agg_rows = (
-        lax.all_to_all(features, "feat", split_axis=1, concat_axis=0, tiled=True),
+        trade_parts(features, "feat", 1, 0),
         lax.all_to_all(aggregate, "feat", split_axis=1, concat_axis=0, tiled=True),
     )
     preact = jnp.einsum("io,iv->ov", weights[0], feat_rows, preferred_element_type=jnp.float32)

time: 259 us -> 258 us (level)
  blocking collectives: 22.9 us -> 0 us
  starting transfers between devices: 37.5 us -> 48.1 us
  local copies, waits for them, and re-layouts: 35.4 us -> 43.4 us
  waiting for transfers between devices: 92.9 us -> 96.1 us
    all_to_all x1 -> x0, blocking collectives: 22.9 us -> none  [pull_mirrors(): lax.all_to_all(outgoing, 'dom', split_axis=1, concat_axis=1, tiled=True)]
    all_to_all x1 -> x2, starting transfers between devices: 11.6 us -> 22 us  [pull_mirrors(): lax.all_to_all(outgoing, 'dom', split_axis=1, concat_axis=1, tiled=True)]
    unnamed x39 -> x48, local copies, waits for them, and re-layouts: 12.5 us -> 21.4 us
    all_to_all x1 -> x2, waiting for transfers between devices: 8.57 us -> 15.4 us  [pull_mirrors(): lax.all_to_all(outgoing, 'dom', split_axis=1, concat_axis=1, tiled=True)]
  transfers between devices with their start and end apart: 7 -> 8, of which waited for: 6 -> 7; matrix products, arithmetic and copies ran while one was open for 22% -> 25% of each run, Pallas kernels for 0% -> 0%
where the time goes in v1:
time: 258 us; the launch traced here: 257 us
  waiting for transfers between devices  96.1 us (37%)
  starting transfers between devices  48.1 us (19%)
  local copies, waits for them, and re-layouts  43.4 us (17%)
  other arithmetic  31.6 us (12%)
  matrix products  22.4 us (9%)
  between operations  15 us (6%)
    all_gather x1, waiting for transfers between devices, local(): grad_cols = lax.all_gather(pre_grad, 'feat', axis=1, tiled=True)  39.7 us
    all_to_all x2, starting transfers between devices, pull_mirrors(): lax.all_to_all(outgoing, 'dom', split_axis=1, concat_axis=1, tiled=True)  22 us
    unnamed x48, local copies, waits for them, and re-layouts  21.4 us
    all_to_all x2, waiting for transfers between devices, push_mirrors(): lax.all_to_all(partial_value[:, masters:].astype(jnp.bfloat16), 'dom', sp...  16.4 us
    scatter-add x2, other arithmetic, push_mirrors(): return partial_value[:, :masters].at[:, targets].add(incoming, mode='drop')  16.4 us
    all_gather x1, waiting for transfers between devices, gathered_total(): pieces = lax.all_gather(x, axis).astype(jnp.float32)  15.6 us
    all_to_all x2, waiting for transfers between devices, pull_mirrors(): lax.all_to_all(outgoing, 'dom', split_axis=1, concat_axis=1, tiled=True)  15.4 us
    all_to_all x1, starting transfers between devices, trade_parts(): received = lax.all_to_all(jnp.stack(pieces), mesh_axis, 0, 0)  10 us
  transfers between devices with their start and end apart: 8, of which 7 were waited for; matrix products, arithmetic and copies ran while one was open for 25% of the time, Pallas kernels for 0%

profile of v1, /device:TPU:1, one launch (start us, length us, event | category | flops | bytes accessed | tf_op | source)
XLA Modules:
  0.0 256.7 jit_solution(17932890263822669511)
XLA Ops:
  7.2 0.9 copy.76
  8.8 1.4 copy.77
  10.1 4.3 %gather_fusion = bf16[1024,64]{1,0:T(8,128)(2,1)} fusion(bf16[64,3072]{0,1:T(8,128)(2,1)S(1)} %copy.77, s32[1024]{0:T(1024)S(1)} %fusion.34), kind=kCustom, calls=%fused_computation.clone | custom fusion | bytes 266240 | tf_op jit(solution)/shard_map/jit(_take)/gather | solution.py:31
  14.4 1.3 bitcast_select_fusion.1
  15.7 0.8 reshape.202
  16.6 11.6 %all-to-all-start.1 = ((bf16[64,2,512]{2,1,0:T(2,128)(2,1)}), bf16[64,2,512]{2,1,0:T(2,128)(2,1)S(1)}, u32[]{:S(2)}, u32[]{:S(2)}) async-start(bf16[64,2,512]{2,1,0:T(2,128)(2,1)} %reshape.202), calls=%async_computation.1 | async-start | bytes 262144 | tf_op jit(solution)/shard_map/all_to_all | solution.py:34
  33.8 5.6 %all-to-all-done.1 = bf16[64,2,512]{2,1,0:T(2,128)(2,1)S(1)} async-done(((bf16[64,2,512]{2,1,0:T(2,128)(2,1)}), bf16[64,2,512]{2,1,0:T(2,128)(2,1)S(1)}, u32[]{:S(2)}, u32[]{:S(2)}) %all-to-all-start.1) | async-done | bytes 131104 | tf_op jit(solution)/shard_map/all_to_all | solution.py:34
  39.8 1.8 gather_fusion.1
  41.7 2.1 convolution_bitcast_fusion.1
  43.7 2.7 %fusion.3 = f32[32,64,128]{2,0,1:T(8,128)S(1)} fusion(f32[64,72,128]{2,0,1:T(8,128)S(1)} %convolution_bitcast_fusion.1, f32[72]{0:T(128)S(1)} %compare_convert_fusion, s32[72]{0:T(128)S(1)} %get-tuple-element.29), kind=kOutput, calls=%fused_computation.11 | convolution fusion | flops 226497024 | bytes 3408448 | tf_op jit(solution)/shard_map/ftd,tb->fbd/dot_general | solution.py:66
  47.0 1.0 copy-done.3
  48.2 0.8 reshape.204
  49.1 4.7 %all-to-all-start.2 = ((bf16[64,2,512]{2,1,0:T(2,128)(2,1)}), bf16[64,2,512]{2,1,0:T(2,128)(2,1)S(1)}, u32[]{:S(2)}, u32[]{:S(2)}) async-start(bf16[64,2,512]{2,1,0:T(2,128)(2,1)} %reshape.204), calls=%async_computation.2 | async-start | bytes 262144 | tf_op jit(solution)/shard_map/all_to_all | solution.py:37
  55.1 9.9 %all-to-all-done.2 = bf16[64,2,512]{2,1,0:T(2,128)(2,1)S(1)} async-done(((bf16[64,2,512]{2,1,0:T(2,128)(2,1)}), bf16[64,2,512]{2,1,0:T(2,128)(2,1)S(1)}, u32[]{:S(2)}, u32[]{:S(2)}) %all-to-all-start.2) | async-done | bytes 131104 | tf_op jit(solution)/shard_map/all_to_all | solution.py:37
  65.0 10.0 %all-to-all-start = ((bf16[8,64,384]{2,1,0:T(8,128)(2,1)}), bf16[8,64,384]{2,1,0:T(8,128)(2,1)}, u32[]{:S(2)}, u32[]{:S(2)}) async-start(bf16[8,64,384]{2,1,0:T(8,128)(2,1)} %bitcast_dynamic-update-slice_fusion), calls=%async_computation | async-start | bytes 786432 | tf_op jit(solution)/shard_map/all_to_all | solution.py:9
  75.7 1.2 slice.50
  76.9 1.7 copy.83
  78.5 1.1 reshape.205
  79.7 8.2 %scatter_custom_fusion = f32[64,3072]{0,1:T(8,128)} fusion(f32[64,3072]{0,1:T(8,128)} %copy.83, s32[1024]{0:T(1024)} %bitcast.147, bf16[64,1024]{0,1:T(8,128)(2,1)S(1)} %bitcast.140), kind=kCustom, calls=%fused_computation.42 | custom fusion | flops 131072 | bytes 917504 | tf_op jit(solution)/shard_map/scatter-add | solution.py:45
  87.8 1.5 convert_element_type.61
  89.3 1.0 copy.84
  90.3 6.6 %all-to-all-start.3 = ((bf16[64,8,384]{2,0,1:T(8,128)(2,1)}), bf16[64,8,384]{2,0,1:T(8,128)(2,1)}, u32[]{:S(2)}, u32[]{:S(2)}) async-start(bf16[64,8,384]{2,0,1:T(8,128)(2,1)} %copy.84), calls=%async_computation.3 | async-start | bytes 786432 | tf_op jit(solution)/shard_map/all_to_all | solution.py:72
  97.2 1.9 copy.85
  99.1 2.4 fusion.19
  101.6 8.9 %all-to-all-done.3 = bf16[64,8,384]{2,0,1:T(8,128)(2,1)} async-done(((bf16[64,8,384]{2,0,1:T(8,128)(2,1)}), bf16[64,8,384]{2,0,1:T(8,128)(2,1)}, u32[]{:S(2)}, u32[]{:S(2)}) %all-to-all-start.3) | async-done | bytes 393248 | tf_op jit(solution)/shard_map/all_to_all | solution.py:72
  110.5 3.1 %multiply_convert_fusion = (bf16[512,384]{0,1:T(8,128)(2,1)}, bf16[512,384]{0,1:T(8,128)(2,1)}) fusion(bf16[512,384]{0,1:T(8,128)(2,1)} %copy.85, f32[384,512]{1,0:T(8,128)} %fusion.19, bf16[512,384]{1,0:T(8,128)(2,1)} %bitcast.26, bf16[2,512,512]{2,1,0:T(8,128)(2,1)} %param.12), kind=kOutput, calls=%fused_computation.30 | convolution fusion | flops 203882496 | bytes 2883584 | tf_op jit(solution)/shard_map/io,iv->ov/dot_general | solution.py:75
  113.6 39.7 %all-gather.3.cloned.1.call-done = bf16[512,3072]{0,1:T(8,128)(2,1)} async-done(((bf16[512,384]{0,1:T(8,128)(2,1)}), bf16[512,3072]{0,1:T(8,128)(2,1)}) %all-gather.3.cloned.1.call-update) | async-done | bytes 3145744 | tf_op jit(solution)/shard_map/all_gather | solution.py:83
  153.3 2.7 %fusion.13 = bf16[1,1,64,512]{3,2,1,0:T(8,128)(2,1)S(1)} fusion(bf16[64,3072]{0,1:T(8,128)(2,1)S(1)} %convert_element_type.61, bf16[512,3072]{0,1:T(8,128)(2,1)} %all-gather.3.cloned.1.call-done), kind=kOutput, calls=%fused_computation.26 | convolution fusion | flops 201359360 | bytes 3604480 | tf_op jit(solution)/shard_map/iv,ov->io/dot_general | solution.py:88
  157.5 3.1 %convolution_convert_fusion = bf16[2,64,3072]{2,1,0:T(8,128)(2,1)S(1)} fusion(bf16[512,3072]{0,1:T(8,128)(2,1)} %all-gather.3.cloned.1.call-done, bf16[2,512,512]{2,1,0:T(8,128)(2,1)} %param.12, s32[]{:T(128)S(6)} %select_n.66), kind=kOutput, calls=%fused_computation.7 | convolution fusion | flops 403046400 | bytes 4063236 | tf_op jit(solution)/shard_map/kio,ov->kiv/dot_general | solution.py:92
  160.7 0.9 copy-done.4
  162.0 4.3 %gather_fusion.2 = bf16[1024,64]{1,0:T(8,128)(2,1)} fusion(bf16[64,3072]{0,1:T(8,128)(2,1)S(1)} %copy.87, s32[1024]{0:T(1024)S(1)} %fusion.34), kind=kCustom, calls=%fused_computation.2.clone | custom fusion | bytes 266240 | tf_op jit(solution)/shard_map/jit(_take)/gather | solution.py:31
  166.3 1.3 bitcast_select_fusion
  168.4 10.4 %all-to-all-start.4 = ((bf16[64,2,512]{2,1,0:T(2,128)(2,1)}), bf16[64,2,512]{2,1,0:T(2,128)(2,1)S(1)}, u32[]{:S(2)}, u32[]{:S(2)}) async-start(bf16[64,2,512]{2,1,0:T(2,128)(2,1)} %reshape.206), calls=%async_computation.4 | async-start | bytes 262144 | tf_op jit(solution)/shard_map/all_to_all | solution.py:34
  178.8 1.9 copy.93
  180.7 9.9 %all-to-all-done.4 = bf16[64,2,512]{2,1,0:T(2,128)(2,1)S(1)} async-done(((bf16[64,2,512]{2,1,0:T(2,128)(2,1)}), bf16[64,2,512]{2,1,0:T(2,128)(2,1)S(1)}, u32[]{:S(2)}, u32[]{:S(2)}) %all-to-all-start.4) | async-done | bytes 131104 | tf_op jit(solution)/shard_map/all_to_all | solution.py:34
  191.1 1.9 gather_fusion.3
  193.0 3.0 %convolution_bitcast_fusion = f32[64,72,128]{2,0,1:T(8,128)S(1)} fusion(bf16[72,128,128]{2,1,0:T(8,128)(2,1)S(1)} %copy-done, bf16[72,64,128]{2,1,0:T(8,128)(2,1)} %gather_fusion.3, pred[72]{0:T(512)(128)(4,1)S(1)} %copy-done.12), kind=kOutput, calls=%fused_computation.13 | convolution fusion | flops 151584768 | bytes 5898312 | tf_op jit(solution)/shard_map/ftd,tsd->fts/dot_general | solution.py:59
  196.0 2.7 %fusion.1 = f32[32,64,128]{2,0,1:T(8,128)S(1)} fusion(f32[64,72,128]{2,0,1:T(8,128)S(1)} %convolution_bitcast_fusion, s32[72]{0:T(128)S(1)} %copy-done.11, f32[72]{0:T(128)S(1)} %copy-done.10), kind=kOutput, calls=%fused_computation.9 | convolution fusion | flops 226497024 | bytes 3408448 | tf_op jit(solution)/shard_map/ftd,tb->fbd/dot_general | solution.py:66
  200.1 1.8 reshape.208
  201.9 4.5 %all-to-all-start.5 = ((bf16[64,2,512]{2,1,0:T(2,128)(2,1)}), bf16[64,2,512]{2,1,0:T(2,128)(2,1)S(1)}, u32[]{:S(2)}, u32[]{:S(2)}) async-start(bf16[64,2,512]{2,1,0:T(2,128)(2,1)} %reshape.208), calls=%async_computation.5 | async-start | bytes 262144 | tf_op jit(solution)/shard_map/all_to_all | solution.py:37
  206.4 2.0 slice_add_fusion
  208.3 2.8 %copy.92 = f32[64,3072]{0,1:T(8,128)} copy(f32[64,3072]{1,0:T(8,128)} %slice_add_fusion) | data formatting | bytes 1572864 | tf_op jit(solution)/shard_map/add
  211.2 6.6 %all-to-all-done.5 = bf16[64,2,512]{2,1,0:T(2,128)(2,1)S(1)} async-done(((bf16[64,2,512]{2,1,0:T(2,128)(2,1)}), bf16[64,2,512]{2,1,0:T(2,128)(2,1)S(1)}, u32[]{:S(2)}, u32[]{:S(2)}) %all-to-all-start.5) | async-done | bytes 131104 | tf_op jit(solution)/shard_map/all_to_all | solution.py:37
  218.0 8.2 %scatter_custom_fusion.1 = f32[64,3072]{0,1:T(8,128)} fusion(f32[64,3072]{0,1:T(8,128)} %copy.92, s32[1024]{0:T(1024)} %bitcast.148, bf16[64,1024]{0,1:T(8,128)(2,1)S(1)} %bitcast.139), kind=kCustom, calls=%fused_computation.40 | custom fusion | flops 131072 | bytes 917504 | tf_op jit(solution)/shard_map/scatter-add | solution.py:45
  226.2 1.5 convert_element_type.70
  227.7 1.0 copy.94
  228.7 15.6 %all-gather.5.cloned.1.call-done = bf16[64,2,64,512]{3,2,1,0:T(8,128)(2,1)} async-done(((bf16[1,2,64,512]{3,2,1,0:T(8,128)(2,1)}), bf16[64,2,64,512]{3,2,1,0:T(8,128)(2,1)}) %all-gather.5.cloned.1.call-update) | async-done | bytes 8388624 | tf_op jit(solution)/shard_map/all_gather | solution.py:14
  244.3 5.5 %convert_reduce_fusion = f32[2,64,512]{2,1,0:T(8,128)} fusion(bf16[64,2,64,512]{3,2,1,0:T(8,128)(2,1)} %all-gather.5.cloned.1.call-done), kind=kLoop, calls=%fused_computation.6 | loop fusion | flops 8323072 | bytes 8650752 | tf_op jit(solution)/shard_map/reduce_sum | solution.py:15
  (64 shorter events, 13.9 us)
Async XLA Ops:
  7.2 34.5 %copy-start = (bf16[72,128,128]{2,1,0:T(8,128)(2,1)S(1)}, bf16[72,128,128]{2,1,0:T(8,128)(2,1)}, u32[]{:S(2)}) copy-start(bf16[72,128,128]{2,1,0:T(8,128)(2,1)} %param.13) | copy-start | bytes 7077892
  7.2 21.0 %copy-start.2 = (bf16[64,3072]{1,0:T(8,128)(2,1)S(1)}, bf16[64,3072]{1,0:T(8,128)(2,1)}, u32[]{:S(2)}) copy-start(bf16[64,3072]{1,0:T(8,128)(2,1)} %param.11) | copy-start | bytes 1179652
  7.2 21.7 %copy-start.8 = (s32[72,2]{0,1:T(2,128)S(1)}, s32[72,2]{0,1:T(2,128)}, u32[]{:S(2)}) copy-start(s32[72,2]{0,1:T(2,128)} %param.14) | copy-start | bytes 1732
  8.1 0.6 copy-start.6
  16.6 22.7 %all-to-all-start.1 = ((bf16[64,2,512]{2,1,0:T(2,128)(2,1)}), bf16[64,2,512]{2,1,0:T(2,128)(2,1)S(1)}, u32[]{:S(2)}, u32[]{:S(2)}) async-start(bf16[64,2,512]{2,1,0:T(2,128)(2,1)} %reshape.202), calls=%async_computation.1 | async-start | bytes 262144 | tf_op jit(solution)/shard_map/all_to_all | solution.py:34
  33.1 10.6 %copy-start.9 = (f32[72]{0:T(128)}, f32[72]{0:T(128)S(1)}, u32[]{:S(2)}) copy-start(f32[72]{0:T(128)S(1)} %compare_convert_fusion) | copy-start | bytes 868
  46.4 28.6 %copy-start.7 = (s32[1,64,16]{2,1,0:T(8,128)S(1)}, s32[1,64,16]{2,1,0:T(8,128)}, u32[]{:S(2)}) copy-start(s32[1,64,16]{2,1,0:T(8,128)} %copy-done.6) | copy-start | bytes 12292
  47.0 1.0 copy-start.3
  49.1 15.9 %all-to-all-start.2 = ((bf16[64,2,512]{2,1,0:T(2,128)(2,1)}), bf16[64,2,512]{2,1,0:T(2,128)(2,1)S(1)}, u32[]{:S(2)}, u32[]{:S(2)}) async-start(bf16[64,2,512]{2,1,0:T(2,128)(2,1)} %reshape.204), calls=%async_computation.2 | async-start | bytes 262144 | tf_op jit(solution)/shard_map/all_to_all | solution.py:37
  65.0 10.1 %copy-start.5 = (bf16[64,2,512]{2,1,0:T(2,128)(2,1)}, bf16[64,2,512]{2,1,0:T(2,128)(2,1)S(1)}, u32[]{:S(2)}) copy-start(bf16[64,2,512]{2,1,0:T(2,128)(2,1)S(1)} %all-to-all-done.2) | copy-start | bytes 393220
  65.0 25.4 %all-to-all-start = ((bf16[8,64,384]{2,1,0:T(8,128)(2,1)}), bf16[8,64,384]{2,1,0:T(8,128)(2,1)}, u32[]{:S(2)}, u32[]{:S(2)}) async-start(bf16[8,64,384]{2,1,0:T(8,128)(2,1)} %bitcast_dynamic-update-slice_fusion), calls=%async_computation | async-start | bytes 786432 | tf_op jit(solution)/shard_map/all_to_all | solution.py:9
  90.3 20.1 %all-to-all-start.3 = ((bf16[64,8,384]{2,0,1:T(8,128)(2,1)}), bf16[64,8,384]{2,0,1:T(8,128)(2,1)}, u32[]{:S(2)}, u32[]{:S(2)}) async-start(bf16[64,8,384]{2,0,1:T(8,128)(2,1)} %copy.84), calls=%async_computation.3 | async-start | bytes 786432 | tf_op jit(solution)/shard_map/all_to_all | solution.py:72
  97.0 56.4 %all-gather.3.cloned.1.call-start = ((), (), s32[]{:S(2)}) async-start(), calls=%async_computation.6 | async-start | bytes 3538944 | tf_op jit(solution)/shard_map/all_gather | solution.py:83
  113.6 130.7 %all-gather.5.cloned.1.call-start = ((), (), s32[]{:S(2)}) async-start(), calls=%async_computation.7 | async-start | bytes 8519680 | tf_op jit(solution)/shard_map/all_gather | solution.py:14
  153.3 2.8 %copy-start.1 = (bf16[512,3072]{0,1:T(8,128)(2,1)S(1)}, bf16[512,3072]{0,1:T(8,128)(2,1)}, u32[]{:S(2)}) copy-start(bf16[512,3072]{0,1:T(8,128)(2,1)} %all-gather.3.cloned.1.call-done) | copy-start | bytes 9437188
  160.7 0.9 copy-start.4
  168.4 22.2 %all-to-all-start.4 = ((bf16[64,2,512]{2,1,0:T(2,128)(2,1)}), bf16[64,2,512]{2,1,0:T(2,128)(2,1)S(1)}, u32[]{:S(2)}, u32[]{:S(2)}) async-start(bf16[64,2,512]{2,1,0:T(2,128)(2,1)} %reshape.206), calls=%async_computation.4 | async-start | bytes 262144 | tf_op jit(solution)/shard_map/all_to_all | solution.py:34
  178.8 14.2 %copy-start.12 = (pred[72]{0:T(512)(128)(4,1)S(1)}, pred[72]{0:T(512)(128)(4,1)}, u32[]{:S(2)}) copy-start(pred[72]{0:T(512)(128)(4,1)} %get-tuple-element.20) | copy-start | bytes 220
  193.0 3.0 %copy-start.10 = (f32[72]{0:T(128)S(1)}, f32[72]{0:T(128)}, u32[]{:S(2)}) copy-start(f32[72]{0:T(128)} %copy-done.9) | copy-start | bytes 868
  193.0 3.0 %copy-start.11 = (s32[72]{0:T(128)S(1)}, s32[72]{0:T(128)}, u32[]{:S(2)}) copy-start(s32[72]{0:T(128)} %get-tuple-element.28) | copy-start | bytes 868
  201.9 15.8 %all-to-all-start.5 = ((bf16[64,2,512]{2,1,0:T(2,128)(2,1)}), bf16[64,2,512]{2,1,0:T(2,128)(2,1)S(1)}, u32[]{:S(2)}, u32[]{:S(2)}) async-start(bf16[64,2,512]{2,1,0:T(2,128)(2,1)} %reshape.208), calls=%async_computation.5 | async-start | bytes 262144 | tf_op jit(solution)/shard_map/all_to_all | solution.py:37
Sparse Core Ops, SparseCore 0:
  113.7 39.6 all-gather.2
  157.6 86.6 all-gather.4
